TPU v7x, 512 devices: a whole 4x8x8 slice. The times are simulated.
512 devices in a mesh: segment: 64 (over z_lo, y, core), head: 8 (over x, z_hi).
Axes of the slice: x: 4, y: 8, z: 8 (z_hi: 2, z_lo: 4; z = z_hi * 4 + z_lo), core: 2. Of those that a mesh axis runs over, the one named last changes fastest.
Arguments:
- segment_rows: bfloat16 [2, 8192, 2048], P(None, 'segment', 'head'), may hold values from -6 to 6
- row_cotangent: bfloat16 [2, 8192, 2048], P(None, 'segment', 'head'), may hold values from -6 to 6
- memory_gain: float32 [2048], P('head'), may hold values from 0.5 to 1.5
- cross_gain: float32 [2048], P('head'), may hold values from 0.5 to 1.5
- w_query: bfloat16 [2048, 2048], P('segment', 'head'), may hold values from -0.125 to 0.125
- w_key: bfloat16 [2048, 2048], P('segment', 'head'), may hold values from -0.125 to 0.125
- w_value: bfloat16 [2048, 2048], P('segment', 'head'), may hold values from -0.125 to 0.125
- w_out: bfloat16 [2048, 2048], P('head', 'segment'), may hold values from -0.125 to 0.125
Outputs:
- segment_result: bfloat16 [2, 8192, 2048], P(None, 'segment', 'head')
All inputs are finite; a program needn't handle non-finite values.
Results may differ from a plain program's by a relative error of at most 0.0065.
Values may be sent and summed in bfloat16 or wider, within the bound.
A program may use at most 64 MiB of HBM per device.

v0:
```python
import jax
import jax.numpy as jnp
from jax import lax
from jax.sharding import PartitionSpec as P

D = 2048
HS = 64


EPS = 1e-06


def shifted(block, axis, distance):
    devices = range(lax.axis_size(axis))
    route = [(i - distance, i) for i in devices if i - distance in devices]
    return lax.ppermute(block, axis, route)


def split_heads(block):
    return block.reshape(block.shape[0], block.shape[1], -1, HS)


def project(block, weight):
    return jnp.einsum("bre,ef->brf", block, weight, preferred_element_type=jnp.float32).astype(
        jnp.bfloat16
    )


def back_project(d_key, d_value, full_key, full_value):
    first = jnp.einsum("brf,ef->bre", d_key, full_key, preferred_element_type=jnp.float32)
    return first + jnp.einsum(
        "brf,ef->bre", d_value, full_value, preferred_element_type=jnp.float32
    )


def attend(normed_all, key_rows, value_rows, cot_all, full_query, full_out):
    batch_count, row_count, _ = normed_all.shape
    factor = HS ** (-0.5)
    query_rows = split_heads(project(normed_all, full_query))
    key_heads = split_heads(key_rows)
    value_heads = split_heads(value_rows)
    scores = (
        jnp.einsum("bqhd,bkhd->bhqk", query_rows, key_heads, preferred_element_type=jnp.float32)
        * factor
    )
    weights_f = jax.nn.softmax(scores, axis=-1)
    weights_low = weights_f.astype(jnp.bfloat16)
    attended = jnp.einsum(
        "bhqk,bkhd->bqhd", weights_low, value_heads, preferred_element_type=jnp.float32
    )
    attended = attended.astype(jnp.bfloat16).reshape(batch_count, row_count, -1)
    out_part = jnp.einsum("brf,fe->bre", attended, full_out, preferred_element_type=jnp.float32)
    d_att = jnp.einsum("bre,fe->brf", cot_all, full_out, preferred_element_type=jnp.float32)
    d_att = split_heads(d_att.astype(jnp.bfloat16))
    d_weights = jnp.einsum(
        "bqhd,bkhd->bhqk", d_att, value_heads, preferred_element_type=jnp.float32
    )
    d_scores = weights_f * (d_weights - jnp.sum(weights_f * d_weights, axis=-1, keepdims=True))
    d_low = (d_scores * factor).astype(jnp.bfloat16)
    d_key = jnp.einsum("bhqk,bqhd->bkhd", d_low, query_rows, preferred_element_type=jnp.float32)
    d_value = jnp.einsum("bhqk,bqhd->bkhd", weights_low, d_att, preferred_element_type=jnp.float32)
    d_key = d_key.astype(jnp.bfloat16).reshape(batch_count, row_count, -1)
    d_value = d_value.astype(jnp.bfloat16).reshape(batch_count, row_count, -1)
    return (out_part, d_key, d_value)


def local(segment_rows, row_cotangent, memory_gain, cross_gain, w_query, w_key, w_value, w_out):
    pair_count = lax.axis_size("segment") // 2
    is_encoder = lax.axis_index("segment") < pair_count
    full_query, full_key, full_value = (
        lax.all_gather(w_query, "segment", axis=0, tiled=True),
        lax.all_gather(w_key, "segment", axis=0, tiled=True),
        lax.all_gather(w_value, "segment", axis=0, tiled=True),
    )
    full_out = lax.all_gather(w_out, "segment", axis=1, tiled=True)
    rows_f = segment_rows.astype(jnp.float32)
    squares = lax.psum(jnp.sum(rows_f * rows_f, axis=-1), "head")
    inv_norm = lax.rsqrt(squares / D + EPS)[..., None]
    gain_here = jnp.where(is_encoder, memory_gain, cross_gain)
    normed = (rows_f * inv_norm * gain_here).astype(jnp.bfloat16)
    memory_here = shifted(normed, "segment", pair_count)
    normed_all, memory_all, cot_all = (
        lax.all_gather(normed, "head", axis=2, tiled=True),
        lax.all_gather(memory_here, "head", axis=2, tiled=True),
        lax.all_gather(row_cotangent, "head", axis=2, tiled=True),
    )
    full_shape = normed_all.shape

    def decoder_work(unused):
        key_rows = project(memory_all, full_key)
        value_rows = project(memory_all, full_value)
        out_part, d_key, d_value = attend(
            normed_all, key_rows, value_rows, cot_all, full_query, full_out
        )
        return (out_part, back_project(d_key, d_value, full_key, full_value))

    def resting(unused):
        return (jnp.zeros(full_shape, jnp.float32), jnp.zeros(full_shape, jnp.float32))

    out_part, memory_part = lax.cond(is_encoder, resting, decoder_work, 0)
    memory_there = shifted(memory_part.astype(jnp.bfloat16), "segment", -pair_count).astype(
        memory_part.dtype
    )
    summed = lax.psum_scatter(
        jnp.where(is_encoder, memory_there, out_part).astype(jnp.bfloat16),
        "head",
        scatter_dimension=2,
        tiled=True,
    ).astype(jnp.float32)
    decoded = (rows_f + summed).astype(jnp.bfloat16)
    weighted = (summed + row_cotangent.astype(jnp.float32)) * gain_here
    inner = lax.psum(jnp.sum(rows_f * weighted, axis=-1), "head")
    d_rows = inv_norm * weighted - rows_f * inv_norm**3 * (inner / D)[..., None]
    return jnp.where(is_encoder, d_rows.astype(jnp.bfloat16), decoded)


def solution(mesh):
    in_specs = (
        P(None, "segment", "head"),
        P(None, "segment", "head"),
        P("head"),
        P("head"),
        P("segment", "head"),
        P("segment", "head"),
        P("segment", "head"),
        P("head", "segment"),
    )
    out_specs = P(None, "segment", "head")
    return jax.shard_map(local, mesh=mesh, in_specs=in_specs, out_specs=out_specs, check_vma=False)
```

profile of v0, /device:TPU:32, one launch (start us, length us, event | category | flops | bytes accessed | tf_op | source)
XLA Modules:
  0.0 897.5 jit_solution(9528429318803133193)
XLA Ops:
  6.5 1.0 fusion.29
  7.6 35.2 %psum.14 = f32[2,128]{1,0:T(2,128)S(1)} all-reduce(f32[2,128]{1,0:T(2,128)S(1)} %fusion.29), channel_id=1, replica_groups=mesh['segment'=64,'head'=8] {'head'}, use_global_device_ids=true, to_apply=%region_1.0 | all-reduce | flops 256 | bytes 2048 | tf_op jit(solution)/shard_map/psum | solution.py:77
  42.7 0.7 broadcast_select_fusion
  43.4 1.7 fusion.31
  45.1 0.0 all-gather.20.cloned.1.call-start
  45.1 0.7 all-gather.20.cloned.1.call-update
  45.9 4.4 collective-permute-start
  50.3 2.8 collective-permute-done
  53.1 0.6 copy-done.9
  53.8 0.0 all-gather.10.cloned.1.call-start
  53.8 0.5 all-gather.10.cloned.1.call-update
  54.3 0.0 all-gather.14.cloned.1.call-start
  54.4 0.5 all-gather.14.cloned.1.call-update
  55.0 0.5 all-gather.16.cloned.1.call-update
  55.6 0.7 all-gather.18.cloned.1.call-update
  56.3 52.5 %all-gather.12.cloned.1.call-done = bf16[2,128,2048]{2,1,0:T(8,128)(2,1)} async-done(((bf16[2,128,256]{2,1,0:T(8,128)(2,1)}), bf16[2,128,2048]{2,1,0:T(8,128)(2,1)}) %all-gather.12.cloned.1.call-update) | async-done | bytes 1048592 | tf_op jit(solution)/shard_map/all_gather | solution.py:83
  108.8 66.4 %all-gather.20.cloned.1.call-done = bf16[2,128,2048]{2,1,0:T(8,128)(2,1)} async-done(((bf16[2,128,256]{2,1,0:T(8,128)(2,1)}), bf16[2,128,2048]{2,1,0:T(8,128)(2,1)}) %all-gather.20.cloned.1.call-update) | async-done | bytes 1048592 | tf_op jit(solution)/shard_map/all_gather | solution.py:85
  175.3 66.5 %all-gather.8.cloned.1.call-done = bf16[2,128,2048]{2,1,0:T(8,128)(2,1)} async-done(((bf16[2,128,256]{2,1,0:T(8,128)(2,1)}), bf16[2,128,2048]{2,1,0:T(8,128)(2,1)}) %all-gather.8.cloned.1.call-update) | async-done | bytes 1048592 | tf_op jit(solution)/shard_map/all_gather | solution.py:84
  241.7 111.1 %all-gather.10.cloned.1.call-done = bf16[2048,256]{1,0:T(8,128)(2,1)} async-done(((bf16[32,256]{1,0:T(8,128)(2,1)}), bf16[2048,256]{1,0:T(8,128)(2,1)}) %all-gather.10.cloned.1.call-update) | async-done | bytes 1048592 | tf_op jit(solution)/shard_map/all_gather | solution.py:73
  352.8 116.6 %all-gather.14.cloned.1.call-done = bf16[2048,256]{1,0:T(8,128)(2,1)} async-done(((bf16[32,256]{1,0:T(8,128)(2,1)}), bf16[2048,256]{1,0:T(8,128)(2,1)}) %all-gather.14.cloned.1.call-update) | async-done | bytes 1048592 | tf_op jit(solution)/shard_map/all_gather | solution.py:71
  469.4 116.6 %all-gather.16.cloned.1.call-done = bf16[2048,256]{1,0:T(8,128)(2,1)} async-done(((bf16[32,256]{1,0:T(8,128)(2,1)}), bf16[2048,256]{1,0:T(8,128)(2,1)}) %all-gather.16.cloned.1.call-update) | async-done | bytes 1048592 | tf_op jit(solution)/shard_map/all_gather | solution.py:72
  585.9 116.7 %all-gather.18.cloned.1.call-done = bf16[256,2048]{0,1:T(8,128)(2,1)} async-done(((bf16[256,32]{0,1:T(8,128)(2,1)}), bf16[256,2048]{0,1:T(8,128)(2,1)}) %all-gather.18.cloned.1.call-update) | async-done | bytes 1048592 | tf_op jit(solution)/shard_map/all_gather | solution.py:75
  702.6 1.2 conditional.1
  702.6 0.1 broadcast.17
  702.8 1.1 broadcast.17.clone
  703.9 1.3 collective-permute-start.1
  705.2 62.9 %collective-permute-done.1 = bf16[2,128,2048]{2,1,0:T(8,128)(2,1)S(1)} collective-permute-done((bf16[2,128,2048]{2,1,0:T(8,128)(2,1)}, bf16[2,128,2048]{2,1,0:T(8,128)(2,1)S(1)}, u32[]{:S(2)}, u32[]{:S(2)}) %collective-permute-start.1) | collective-permute-done | bytes 1048608 | tf_op jit(solution)/shard_map/ppermute | solution.py:16
  768.1 1.4 select_convert_fusion
  769.5 93.1 %reduce-scatter.2.cloned.1.call-done = bf16[2,128,256]{2,1,0:T(8,128)(2,1)} async-done(((bf16[2,128,2048]{2,1,0:T(8,128)(2,1)}), bf16[2,128,256]{2,1,0:T(8,128)(2,1)}) %reduce-scatter.2.cloned.1.call-update) | async-done | bytes 131088 | tf_op jit(solution)/shard_map/reduce_scatter | solution.py:104
  862.6 1.0 fusion.35
  863.7 25.2 %psum.15 = f32[2,128]{1,0:T(2,128)S(1)} all-reduce(f32[2,128]{1,0:T(2,128)S(1)} %fusion.35), channel_id=1, replica_groups=mesh['segment'=64,'head'=8] {'head'}, use_global_device_ids=true, to_apply=%region_9.10 | all-reduce | flops 256 | bytes 2048 | tf_op jit(solution)/shard_map/psum | solution.py:112
  888.9 1.7 fusion.37
  (15 shorter events, 0.2 us)
Async XLA Ops:
  6.5 102.3 %all-gather.12.cloned.1.call-start = ((), (), s32[]{:S(2)}) async-start(), calls=%async_computation.3 | async-start | bytes 1179648 | tf_op jit(solution)/shard_map/all_gather | solution.py:83
  45.1 130.2 %all-gather.20.cloned.1.call-start = ((), (), s32[]{:S(2)}) async-start(), calls=%async_computation.7 | async-start | bytes 1179648 | tf_op jit(solution)/shard_map/all_gather | solution.py:85
  45.9 195.9 %all-gather.8.cloned.1.call-start = ((), (), s32[]{:S(2)}) async-start(), calls=%async_computation.1 | async-start | bytes 1179648 | tf_op jit(solution)/shard_map/all_gather | solution.py:84
  45.9 7.2 collective-permute-start
  53.1 0.7 copy-start.9
  53.8 299.1 %all-gather.10.cloned.1.call-start = ((), (), s32[]{:S(2)}) async-start(), calls=%async_computation.2 | async-start | bytes 1064960 | tf_op jit(solution)/shard_map/all_gather | solution.py:73
  54.3 415.0 %all-gather.14.cloned.1.call-start = ((), (), s32[]{:S(2)}) async-start(), calls=%async_computation.4 | async-start | bytes 1064960 | tf_op jit(solution)/shard_map/all_gather | solution.py:71
  54.9 531.0 %all-gather.16.cloned.1.call-start = ((), (), s32[]{:S(2)}) async-start(), calls=%async_computation.5 | async-start | bytes 1064960 | tf_op jit(solution)/shard_map/all_gather | solution.py:72
  55.5 647.1 %all-gather.18.cloned.1.call-start = ((), (), s32[]{:S(2)}) async-start(), calls=%async_computation.6 | async-start | bytes 1064960 | tf_op jit(solution)/shard_map/all_gather | solution.py:75
  56.3 806.3 %reduce-scatter.2.cloned.1.call-start = ((), (), s32[]{:S(2)}) async-start(), calls=%async_computation.8 | async-start | bytes 1179648 | tf_op jit(solution)/shard_map/reduce_scatter | solution.py:104
  703.9 64.2 %collective-permute-start.1 = (bf16[2,128,2048]{2,1,0:T(8,128)(2,1)}, bf16[2,128,2048]{2,1,0:T(8,128)(2,1)S(1)}, u32[]{:S(2)}, u32[]{:S(2)}) collective-permute-start(bf16[2,128,2048]{2,1,0:T(8,128)(2,1)} %get-tuple-element.28), channel_id=1, source_target_pairs={{256,0},{264,8},{272,16},{280,24},{288,32},{296,40},{304,48},{312,... | collective-permute-start | bytes 3145736 | tf_op jit(solution)/shard_map/ppermute | solution.py:16
  768.1 94.5 %copy-start.6 = (bf16[2,128,256]{2,1,0:T(8,128)(2,1)S(1)}, bf16[2,128,256]{2,1,0:T(8,128)(2,1)}, u32[]{:S(2)}) copy-start(bf16[2,128,256]{2,1,0:T(8,128)(2,1)} %param.10) | copy-start | bytes 393220
  768.1 94.5 %copy-start.7 = (bf16[2,128,256]{2,1,0:T(8,128)(2,1)S(1)}, bf16[2,128,256]{2,1,0:T(8,128)(2,1)}, u32[]{:S(2)}) copy-start(bf16[2,128,256]{2,1,0:T(8,128)(2,1)} %param.11) | copy-start | bytes 393220
Sparse Core Ops, SparseCore 0:
  45.2 63.5 all-gather.11
  111.9 63.3 all-gather.19
  178.3 63.3 all-gather.7
  243.7 109.0 all-gather.9
  354.8 114.5 all-gather.13
  471.4 114.5 all-gather.15
  588.1 114.5 all-gather.17
  769.6 92.9 reduce-scatter.1
where the time goes:
time: 898 us; the launch traced here: 897 us
  waiting for transfers between devices  808 us (90%)
  blocking collectives  60.4 us (7%)
  between operations  13.5 us (2%)
    all_gather x1, waiting for transfers between devices, local(): full_out = lax.all_gather(w_out, 'segment', axis=1, tiled=True)  117 us
    all_gather x1, waiting for transfers between devices, local(): lax.all_gather(w_key, 'segment', axis=0, tiled=True)  117 us
    all_gather x1, waiting for transfers between devices, local(): lax.all_gather(w_query, 'segment', axis=0, tiled=True)  117 us
    all_gather x1, waiting for transfers between devices, local(): lax.all_gather(w_value, 'segment', axis=0, tiled=True)  111 us
    reduce_scatter x1, waiting for transfers between devices, local(): lax.psum_scatter(jnp.where(is_encoder, memory_there, out_part).astype(jnp...  93.1 us
    all_gather x1, waiting for transfers between devices, local(): lax.all_gather(memory_here, 'head', axis=2, tiled=True)  66.5 us
    all_gather x1, waiting for transfers between devices, local(): lax.all_gather(row_cotangent, 'head', axis=2, tiled=True)  66.4 us
    ppermute x2, waiting for transfers between devices, shifted(): return lax.ppermute(block, axis, route)  65.7 us
  transfers between devices with their start and end apart: 10, of which 10 were waited for; matrix products, arithmetic and copies ran while one was open for 0% of the time, Pallas kernels for 0%

commit v1 on v0

v1 whole, which is shorter than its diff:
```python
import functools

import jax
import jax.numpy as jnp
from jax import lax
from jax.experimental import pallas as pl
from jax.experimental.pallas import tpu as pltpu
from jax.sharding import PartitionSpec as P

D = 2048
HS = 64
EPS = 1e-06
NX = 4
NY = 8
NT = (((1,), (1,)), ((), ()))
TN = (((0,), (0,)), ((), ()))
F32 = jnp.float32
BF16 = jnp.bfloat16

W_Z = 0
W_RIGHT = 3
W_LEFT = 19
W_MATE = 35
A_ROWS = 43
A_COT = 46
A_AUX = 49
A_RIGHT = 52
A_LEFT = 55
X_AUX = 58
S_OUT = 61
S_STAT = 73
F_SUM = 76
F_STAT = 79
COPIES = 82


def dot(a, b, dims=(((1,), (0,)), ((), ()))):
    return lax.dot_general(a, b, dims, preferred_element_type=F32)


def kernel(
    rows, cot, mgain, cgain, wq, wk, wv, wo, out,
    w, act, aux, hold, stage, near, far, stat_out, stat_in, last, last_in, last_stat, stat_last,
    ssem, rsem,
):
    seg = lax.axis_index("segment")
    head = lax.axis_index("head")
    c = seg % 2
    y = (seg // 2) % NY
    zl = seg // (2 * NY)
    p = zl % 2
    side = zl // 2
    x = head // 2
    zh = head % 2
    oh = 1 - zh
    other = 1 - side

    def at(x_=x, y_=y, zl_=zl, zh_=zh, c_=c):
        return ((zl_ * NY + y_) * 2 + c_, x_ * 2 + zh_)

    xr, xl, xx = (x + 1) % NX, (x + NX - 1) % NX, (x + 2) % NX
    right, left, across = at(x_=xr), at(x_=xl), at(x_=xx)
    up, down = at(y_=(y + 1) % NY), at(y_=(y + NY - 1) % NY)
    mate = at(c_=1 - c)
    zl_of = (zl, (1 - p) + 2 * side, p + 2 * other, (1 - p) + 2 * other)
    w_to = [None] + [at(zl_=v) for v in zl_of[1:]]
    r1, r2, r3 = at(zl_=zl_of[2]), at(zh_=oh), at(zl_=zl_of[2], zh_=oh)

    def copy(src, dst, number, to):
        return pltpu.make_async_remote_copy(
            src_ref=src, dst_ref=dst, send_sem=ssem.at[number], recv_sem=rsem.at[number],
            device_id=to, device_id_type=pl.DeviceIdType.MESH,
        )

    pending = []

    def send(src, dst, number, to):
        one = copy(src, dst, number, to)
        one.start()
        pending.append(one)

    def arrived(dst, number):
        copy(dst, dst, number, mate).wait_recv()

    eye = lax.broadcasted_iota(jnp.int32, (128, 128), 0) == lax.broadcasted_iota(
        jnp.int32, (128, 128), 1
    )

    def as_row(col):
        return jnp.sum(jnp.where(eye, col, 0.0), axis=0, keepdims=True)

    def as_col(row):
        return jnp.sum(jnp.where(eye, row, 0.0), axis=1, keepdims=True)

    barrier = pltpu.get_barrier_semaphore()
    partners = (right, left, across, up, down, mate, r1, r2, r3, w_to[1], w_to[3])
    for partner in partners:
        pl.semaphore_signal(
            barrier, inc=1, device_id=partner, device_id_type=pl.DeviceIdType.MESH
        )
    w[zl, y, c, :, 0:256] = wq[...]
    w[zl, y, c, :, 256:512] = wk[...]
    w[zl, y, c, :, 512:768] = wv[...]
    w[zl, y, c, :, 768:1024] = jnp.transpose(wo[...].astype(F32)).astype(BF16)
    act[side, x, zh] = rows[side]

    @pl.when(side == 1)
    def _():
        act[2, x, zh] = cot[1]

    @pl.when(side == 0)
    def _():
        aux[x, zh, 0:1, :] = mgain[...]
        aux[x, zh, 1:2, :] = cgain[...]
        for m in range(2):
            inner = rows[m].astype(F32) * cot[m].astype(F32) * mgain[...]
            aux[x, zh, 2:3, 128 * m : 128 * m + 128] = as_row(
                jnp.sum(inner, axis=1, keepdims=True)
            )
        aux[x, zh, 3:8, :] = jnp.zeros((5, 256), F32)

    pl.semaphore_wait(barrier, len(partners))

    own = w.at[zl, y, c]
    for d in (2, 1, 3):
        send(own, own, W_Z + d - 1, w_to[d])
    send(own, own, W_RIGHT, up)
    send(own, own, W_LEFT, down)

    mine = act.at[side, x, zh]
    send(rows.at[other], mine, A_ROWS, r1)
    send(rows.at[other], mine, A_ROWS + 2, r3)
    send(rows.at[side], mine, A_ROWS + 1, r2)
    my_cot = act.at[2, x, zh]
    my_aux = aux.at[x, zh]
    cots = [
        copy(cot.at[0], my_cot, A_COT, r1),
        copy(cot.at[0], my_cot, A_COT + 2, r3),
        copy(cot.at[1], my_cot, A_COT + 1, r2),
    ]
    auxes = [copy(my_aux, my_aux, A_AUX + i, to) for i, to in enumerate((r1, r2, r3))]

    @pl.when(side == 1)
    def _():
        for one in cots:
            one.start()

    @pl.when(side == 0)
    def _():
        for one in auxes:
            one.start()

    def up_down(t, d):
        if t < 4 or d < 2:
            block = w.at[zl_of[d], (y + NY - t + 1) % NY, c]
            send(block, block, W_RIGHT + 4 * (t - 1) + d, up)
        if t < 4 or d >= 2:
            block = w.at[zl_of[d], (y + t - 1) % NY, c]
            send(block, block, W_LEFT + 4 * (t - 1) + d, down)

    def from_ring(t, d):
        if t < 4 or d < 2:
            arrived(w.at[zl_of[d], (y + NY - t) % NY, c], W_RIGHT + 4 * (t - 1) + d)
        if t < 4 or d >= 2:
            arrived(w.at[zl_of[d], (y + t) % NY, c], W_LEFT + 4 * (t - 1) + d)

    def share(number):
        block = w.at[:, (y + number) % NY, c]
        send(block, block, W_MATE + number, mate)

    for d in (1, 2, 3):
        arrived(w.at[zl_of[d], y, c], W_Z + d - 1)
        up_down(1, d)
    share(0)

    def group(x_, g):
        return act.at[:, x_, oh if g else zh]

    arrived(act.at[other, x, zh], A_ROWS)

    @pl.when(side == 0)
    def _():
        arrived(act.at[2, x, zh], A_COT)

    send(group(x, 0), group(x, 0), A_RIGHT, right)
    send(group(x, 0), group(x, 0), A_LEFT, left)
    arrived(act.at[side, x, oh], A_ROWS + 1)
    arrived(act.at[other, x, oh], A_ROWS + 2)

    @pl.when(side == 0)
    def _():
        arrived(act.at[2, x, oh], A_COT + 2)
        arrived(aux.at[x, oh], A_AUX + 1)

    @pl.when(side == 1)
    def _():
        arrived(act.at[2, x, oh], A_COT + 1)
        arrived(aux.at[x, zh], A_AUX)
        arrived(aux.at[x, oh], A_AUX + 2)

    send(group(x, 1), group(x, 1), A_RIGHT + 1, right)
    send(group(x, 1), group(x, 1), A_LEFT + 1, left)
    for i, to in enumerate((right, left, across)):
        send(aux.at[x], aux.at[x], X_AUX + i, to)

    for d in range(4):
        from_ring(1, d)
        up_down(2, d)
    share(1)
    share(7)

    arrived(group(xl, 0), A_RIGHT)
    send(group(xl, 0), group(xl, 0), A_RIGHT + 2, right)
    arrived(group(xr, 0), A_LEFT)
    arrived(group(xl, 1), A_RIGHT + 1)
    arrived(group(xr, 1), A_LEFT + 1)
    send(group(xr, 1), group(xr, 1), A_LEFT + 2, left)

    for d in range(4):
        from_ring(2, d)
        up_down(3, d)
    share(2)
    share(6)
    for d in range(4):
        from_ring(3, d)
        up_down(4, d)
    share(3)
    share(5)
    for d in range(4):
        from_ring(4, d)
    share(4)

    arrived(group(xx, 0), A_RIGHT + 2)
    arrived(group(xx, 1), A_LEFT + 2)
    for i, x_ in enumerate((xl, xr, xx)):
        arrived(aux.at[x_], X_AUX + i)
    for number in range(NY):
        arrived(w.at[:, (y + number) % NY, 1 - c], W_MATE + number)

    blocks = [(i // 2, i % 2) for i in range(8)]

    def inverse(kind):
        total = jnp.zeros((128, 256), F32)
        for i, j in blocks:
            v = act[kind, i, j].astype(F32)
            total = total + v * v
        return lax.rsqrt(jnp.sum(total, axis=1, keepdims=True) / D + EPS)

    inv_e = inverse(0)
    inv_x = inverse(1)
    kv = jnp.zeros((128, 512), F32)
    q = jnp.zeros((128, 256), F32)
    da = jnp.zeros((128, 256), F32)
    c_inner = jnp.zeros((1, 256), F32)
    for i, j in blocks:
        memory = (act[0, i, j].astype(F32) * inv_e * aux[i, j, 0:1, :]).astype(BF16)
        normed = (act[1, i, j].astype(F32) * inv_x * aux[i, j, 1:2, :]).astype(BF16)
        part = w.at[i, 4 * j : 4 * j + 4]
        kv = kv + dot(memory, part[:, :, :, 256:768].reshape(256, 512))
        q = q + dot(normed, part[:, :, :, 0:256].reshape(256, 256))
        da = da + dot(act[2, i, j], part[:, :, :, 768:1024].reshape(256, 256))
        c_inner = c_inner + aux[i, j, 2:3, :]
    kv = kv.astype(BF16).astype(F32)
    q = q.astype(BF16).astype(F32)
    da = da.astype(BF16).astype(F32)
    c_inner = jnp.where(side == 0, c_inner[:, 0:128], c_inner[:, 128:256])

    low = lax.broadcasted_iota(jnp.int32, (128, 128), 1) < HS
    factor = HS ** (-0.5)

    def two(v):
        return jnp.concatenate(
            [jnp.where(low, v, 0.0).astype(BF16), jnp.where(low, 0.0, v).astype(BF16)], axis=0
        )

    attended, saved = [], []
    for pair in range(2):
        lanes = slice(128 * pair, 128 * pair + 128)
        q2 = two(q[:, lanes])
        key = kv[:, lanes].astype(BF16)
        value = kv[:, 256 + 128 * pair : 384 + 128 * pair]
        scores = dot(q2, key, NT) * factor
        e = jnp.exp(scores - jnp.max(scores, axis=1, keepdims=True))
        probs = e / jnp.sum(e, axis=1, keepdims=True)
        probs_low = probs.astype(BF16)
        v2 = two(value)
        attended.append(dot(probs_low[:128], v2[:128]) + dot(probs_low[128:], v2[128:]))
        saved.append((q2, value.astype(BF16), probs, probs_low, two(da[:, lanes])))
    attended = jnp.concatenate(attended, axis=1).astype(BF16)

    def weight_rows(x_, j, lanes):
        return w[x_, 4 * j : 4 * j + 4, :, :, lanes].reshape(256, lanes.stop - lanes.start)

    def hand_out(kind, chunk):
        base = S_OUT + 6 * kind
        stage[kind, 0] = chunk(xx, 0).astype(BF16)
        send(stage.at[kind, 0], far.at[kind, 0], base, right)
        stage[kind, 1] = chunk(xx, 1).astype(BF16)
        send(stage.at[kind, 1], far.at[kind, 1], base + 1, left)
        stage[kind, 2] = chunk(xr, 1).astype(BF16)
        send(stage.at[kind, 2], near.at[kind, 0], base + 2, right)
        stage[kind, 3] = chunk(xl, 0).astype(BF16)
        send(stage.at[kind, 3], near.at[kind, 1], base + 3, left)
        hold[kind, 0] = chunk(xr, 0)
        hold[kind, 1] = chunk(xl, 1)
        hold[kind, 2] = chunk(x, 0)
        hold[kind, 3] = chunk(x, 1)

    def pass_on(kind):
        base = S_OUT + 6 * kind
        for i, to in enumerate((right, left)):
            arrived(far.at[kind, i], base + i)
            stage[kind, 4 + i] = (hold[kind, i] + far[kind, i].astype(F32)).astype(BF16)
            send(stage.at[kind, 4 + i], near.at[kind, 2 + i], base + 4 + i, to)

    def finish(kind):
        base = S_OUT + 6 * kind
        for i in range(4):
            arrived(near.at[kind, i], base + 2 + i)
        hold[kind, 2] = hold[kind, 2] + near[kind, 2].astype(F32) + near[kind, 1].astype(F32)
        hold[kind, 3] = hold[kind, 3] + near[kind, 0].astype(F32) + near[kind, 3].astype(F32)
        for i in range(2):
            last[kind, i] = hold[kind, 2 + i].astype(BF16)

    hand_out(1, lambda x_, j: dot(attended, weight_rows(x_, j, slice(768, 1024)), NT))

    d_keys, d_values = [], []
    for q2, value, probs, probs_low, da2 in saved:
        d_probs = dot(da2, value, NT)
        d_scores = probs * (d_probs - jnp.sum(probs * d_probs, axis=1, keepdims=True))
        d_low = (d_scores * factor).astype(BF16)
        d_keys.append(dot(d_low, q2, TN))
        d_values.append(dot(probs_low, da2, TN))
    d_kv = jnp.concatenate(d_keys + d_values, axis=1).astype(BF16)
    pass_on(1)

    inner = [jnp.zeros((128, 256), F32)]

    def memory_chunk(x_, j):
        v = dot(d_kv, weight_rows(x_, j, slice(256, 768)), NT)
        inner[0] = inner[0] + v * (act[0, x_, j].astype(F32) * aux[x_, j, 0:1, :])
        return v

    hand_out(0, memory_chunk)
    own_inner = as_row(jnp.sum(inner[0], axis=1, keepdims=True))
    stat_out[0:1, :] = own_inner
    stat_out[1:8, :] = jnp.zeros((7, 128), F32)
    for i, to in enumerate((right, left, across)):
        send(stat_out, stat_in.at[i], S_STAT + i, to)
    pass_on(0)

    cross = [
        copy(last.at[other, zh], last_in.at[0], F_SUM, r1),
        copy(last.at[other, oh], last_in.at[2], F_SUM + 2, r3),
    ]
    same = copy(last.at[side, oh], last_in.at[1], F_SUM + 1, r2)

    def to_owner(kind):
        @pl.when(side == kind)
        def _():
            same.start()

        @pl.when(side != kind)
        def _():
            for one in cross:
                one.start()

    finish(1)
    to_owner(1)
    for i in range(3):
        arrived(stat_in.at[i], S_STAT + i)
    part_inner = own_inner
    for i in range(3):
        part_inner = part_inner + stat_in[i, 0:1, :]
    part_inner = part_inner + jnp.where(zh == 0, c_inner, 0.0)
    last_stat[0:1, :] = part_inner
    last_stat[1:2, :] = as_row(inv_e)
    last_stat[2:8, :] = jnp.zeros((6, 128), F32)
    for i, to in enumerate((r1, r2, r3)):
        send(last_stat, stat_last.at[i], F_STAT + i, to)
    finish(0)
    to_owner(0)

    for i in range(3):
        arrived(stat_last.at[i], F_STAT + i)
        arrived(last_in.at[i], F_SUM + i)
    sums = (
        hold[side, 2 + zh] + last_in[1].astype(F32),
        last_in[0].astype(F32) + last_in[2].astype(F32),
    )

    @pl.when(side == 1)
    def _():
        for m, total in ((1, sums[0]), (0, sums[1])):
            out[m] = (rows[m].astype(F32) + total).astype(BF16)

    @pl.when(side == 0)
    def _():
        inners = (
            part_inner + stat_last[1, 0:1, :],
            stat_last[0, 0:1, :] + stat_last[2, 0:1, :],
        )
        invs = (inv_e, as_col(stat_last[0, 1:2, :]))
        for m in range(2):
            weighted = (sums[m] + cot[m].astype(F32)) * mgain[...]
            mean = as_col(inners[m]) / D
            inv = invs[m]
            d_rows = inv * weighted - rows[m].astype(F32) * (inv * inv * inv * mean)
            out[m] = d_rows.astype(BF16)

    for one in pending:
        one.wait_send()
    same.wait_send()
    for one in cross:
        one.wait_send()

    @pl.when(side == 1)
    def _():
        for one in cots:
            one.wait_send()

    @pl.when(side == 0)
    def _():
        for one in auxes:
            one.wait_send()


def local(segment_rows, row_cotangent, memory_gain, cross_gain, w_query, w_key, w_value, w_out):
    vmem = pl.BlockSpec(memory_space=pltpu.VMEM)
    return pl.pallas_call(
        kernel,
        out_shape=jax.ShapeDtypeStruct((2, 128, 256), BF16),
        in_specs=[vmem] * 8,
        out_specs=vmem,
        scratch_shapes=[
            pltpu.VMEM((4, NY, 2, 32, 1024), BF16),
            pltpu.VMEM((3, NX, 2, 128, 256), BF16),
            pltpu.VMEM((NX, 2, 8, 256), F32),
            pltpu.VMEM((2, 4, 128, 256), F32),
            pltpu.VMEM((2, 6, 128, 256), BF16),
            pltpu.VMEM((2, 4, 128, 256), BF16),
            pltpu.VMEM((2, 2, 128, 256), BF16),
            pltpu.VMEM((8, 128), F32),
            pltpu.VMEM((3, 8, 128), F32),
            pltpu.VMEM((2, 2, 128, 256), BF16),
            pltpu.VMEM((3, 128, 256), BF16),
            pltpu.VMEM((8, 128), F32),
            pltpu.VMEM((3, 8, 128), F32),
            pltpu.SemaphoreType.DMA((COPIES,)),
            pltpu.SemaphoreType.DMA((COPIES,)),
        ],
        compiler_params=pltpu.CompilerParams(
            collective_id=0, has_side_effects=True, vmem_limit_bytes=48 * 1024 * 1024
        ),
    )(
        segment_rows, row_cotangent, memory_gain.reshape(1, -1), cross_gain.reshape(1, -1),
        w_query, w_key, w_value, w_out,
    )


def solution(mesh):
    in_specs = (
        P(None, "segment", "head"),
        P(None, "segment", "head"),
        P("head"),
        P("head"),
        P("segment", "head"),
        P("segment", "head"),
        P("segment", "head"),
        P("head", "segment"),
    )
    out_specs = P(None, "segment", "head")
    return jax.shard_map(local, mesh=mesh, in_specs=in_specs, out_specs=out_specs, check_vma=False)
```

time: 898 us -> 77.7 us (0.09)
  the two profiles are of different devices: /device:TPU:32 before, /device:TPU:19 now
where the time goes in v1:
time: 77.7 us; the launch traced here: 77.5 us
  Pallas kernels  74 us (95%)
  local copies, waits for them, and re-layouts  3.36 us (4%)
    pallas_call x1, Pallas kernels, local(): pl.pallas_call(kernel, out_shape=jax.ShapeDtypeStruct((2, 128, 256), BF16...  74 us
    unnamed x16, local copies, waits for them, and re-layouts  3.36 us

profile of v1, /device:TPU:19, one launch (start us, length us, event | category | flops | bytes accessed | tf_op | source)
XLA Modules:
  0.0 77.5 jit_solution(1388423872173380351)
XLA Ops:
  0.0 0.0 copy-start.2
  0.0 0.0 copy-start.3
  0.0 0.0 copy-start.4
  0.0 0.0 copy-start.5
  0.0 0.0 copy-start.6
  0.0 0.9 %copy.9.wo = bf16[256,32]{1,0:T(8,128)(2,1)S(1)} copy(bf16[256,32]{0,1:T(8,128)(2,1)} %param.15) | data formatting | bytes 32768 | tf_op args[7]
  0.9 0.0 copy-done.2
  0.9 0.0 copy-done.3
  0.9 0.0 copy-done.4
  0.9 0.0 copy-done.5
  1.0 0.0 copy-done.6
  1.0 0.0 copy-start
  1.0 0.9 %copy-done = bf16[2,128,256]{2,1,0:T(8,128)(2,1)S(1)} copy-done((bf16[2,128,256]{2,1,0:T(8,128)(2,1)S(1)}, bf16[2,128,256]{2,1,0:T(8,128)(2,1)}, u32[]{:S(2)}) %copy-start) | copy-done | bytes 131096
  1.9 0.0 copy-start.1
  1.9 0.9 %copy-done.1 = bf16[2,128,256]{2,1,0:T(8,128)(2,1)S(1)} copy-done((bf16[2,128,256]{2,1,0:T(8,128)(2,1)S(1)}, bf16[2,128,256]{2,1,0:T(8,128)(2,1)}, u32[]{:S(2)}) %copy-start.1) | copy-done | bytes 131096
  2.8 74.0 %shard_map.82 = bf16[2,128,256]{2,1,0:T(8,128)(2,1)S(1)} custom-call(bf16[2,128,256]{2,1,0:T(8,128)(2,1)S(1)} %copy-done, bf16[2,128,256]{2,1,0:T(8,128)(2,1)S(1)} %copy-done.1, f32[1,256]{1,0:T(1,128)S(1)} %bitcast.2, f32[1,256]{1,0:T(1,128)S(1)} %bitcast.3, bf16[32,256]{1,0:T(8,128)(2,1)S(1)} %copy-done.2, bf16[32,256]{1,0:T(8,128)(2,1)S(1)} %copy-done.3, ...), custom_call_target="tpu_custom_call" | custom-call | tf_op jit(solution)/shard_map/pallas_call | solution.py:430
  76.8 0.7 copy.11
Async XLA Ops:
  0.0 0.9 %copy-start.2 = (bf16[32,256]{1,0:T(8,128)(2,1)S(1)}, bf16[32,256]{1,0:T(8,128)(2,1)}, u32[]{:S(2)}) copy-start(bf16[32,256]{1,0:T(8,128)(2,1)} %wq.1) | copy-start | bytes 49156
  0.0 0.9 %copy-start.3 = (bf16[32,256]{1,0:T(8,128)(2,1)S(1)}, bf16[32,256]{1,0:T(8,128)(2,1)}, u32[]{:S(2)}) copy-start(bf16[32,256]{1,0:T(8,128)(2,1)} %wk.1) | copy-start | bytes 49156
  0.0 0.9 %copy-start.4 = (bf16[32,256]{1,0:T(8,128)(2,1)S(1)}, bf16[32,256]{1,0:T(8,128)(2,1)}, u32[]{:S(2)}) copy-start(bf16[32,256]{1,0:T(8,128)(2,1)} %wv.1) | copy-start | bytes 49156
  0.0 0.9 %copy-start.5 = (f32[256]{0:T(256)S(1)}, f32[256]{0:T(256)}, u32[]{:S(2)}) copy-start(f32[256]{0:T(256)} %param.10) | copy-start | bytes 3076
  0.0 0.9 %copy-start.6 = (f32[256]{0:T(256)S(1)}, f32[256]{0:T(256)}, u32[]{:S(2)}) copy-start(f32[256]{0:T(256)} %param.11) | copy-start | bytes 3076
  1.0 0.9 %copy-start = (bf16[2,128,256]{2,1,0:T(8,128)(2,1)S(1)}, bf16[2,128,256]{2,1,0:T(8,128)(2,1)}, u32[]{:S(2)}) copy-start(bf16[2,128,256]{2,1,0:T(8,128)(2,1)} %rows.1) | copy-start | bytes 393220
  1.9 0.9 %copy-start.1 = (bf16[2,128,256]{2,1,0:T(8,128)(2,1)S(1)}, bf16[2,128,256]{2,1,0:T(8,128)(2,1)}, u32[]{:S(2)}) copy-start(bf16[2,128,256]{2,1,0:T(8,128)(2,1)} %cot.1) | copy-start | bytes 393220

commit v2 on v1

v2 whole, which is shorter than its diff:
```python
import functools

import jax
import jax.numpy as jnp
from jax import lax
from jax.experimental import pallas as pl
from jax.experimental.pallas import tpu as pltpu
from jax.sharding import PartitionSpec as P

D = 2048
HS = 64
EPS = 1e-06
NX = 4
NY = 8
NT = (((1,), (1,)), ((), ()))
TN = (((0,), (0,)), ((), ()))
F32 = jnp.float32
BF16 = jnp.bfloat16

Q_Z = 0
Q_UP = 3
Q_DOWN = 19
Q_MATE = 35
O_Z = 43
O_UP = 46
O_DOWN = 50
O_MATE = 54
A_ROWS = 62
A_COT = 65
A_AUX = 68
X_ROWS = 71
X_COT = 83
X_AUX = 95
S_OUT = 98
S_STAT = 110
F_SUM = 113
F_STAT = 116
COPIES = 119


def dot(a, b, dims=(((1,), (0,)), ((), ()))):
    return lax.dot_general(a, b, dims, preferred_element_type=F32)


def kernel(
    rows_h, cot_h, mgain_h, cgain_h, wq, wk, wv, wo, out,
    rows, cot, gains, wa, wb, act, aux, hold, stage, near, far, stat_out, stat_in, last, last_in, last_stat,
    stat_last, lsem, ssem, rsem,
):
    seg = lax.axis_index("segment")
    head = lax.axis_index("head")
    c = seg % 2
    y = (seg // 2) % NY
    zl = seg // (2 * NY)
    p = zl % 2
    side = zl // 2
    x = head // 2
    zh = head % 2
    oh = 1 - zh
    other = 1 - side

    def at(x_=x, y_=y, zl_=zl, zh_=zh, c_=c):
        return ((zl_ * NY + y_) * 2 + c_, x_ * 2 + zh_)

    xr, xl, xx = (x + 1) % NX, (x + NX - 1) % NX, (x + 2) % NX
    right, left, across = at(x_=xr), at(x_=xl), at(x_=xx)
    up, down = at(y_=(y + 1) % NY), at(y_=(y + NY - 1) % NY)
    mate = at(c_=1 - c)
    zl_of = (zl, (1 - p) + 2 * side, p + 2 * other, (1 - p) + 2 * other)
    w_to = [None] + [at(zl_=v) for v in zl_of[1:]]
    r1, r2, r3 = at(zl_=zl_of[2]), at(zh_=oh), at(zl_=zl_of[2], zh_=oh)

    def copy(src, dst, number, to):
        return pltpu.make_async_remote_copy(
            src_ref=src, dst_ref=dst, send_sem=ssem.at[number], recv_sem=rsem.at[number],
            device_id=to, device_id_type=pl.DeviceIdType.MESH,
        )

    pending = []

    def send(src, dst, number, to):
        one = copy(src, dst, number, to)
        one.start()
        pending.append(one)

    def arrived(dst, number):
        copy(dst, dst, number, mate).wait_recv()

    eye = lax.broadcasted_iota(jnp.int32, (128, 128), 0) == lax.broadcasted_iota(
        jnp.int32, (128, 128), 1
    )

    def as_row(col):
        return jnp.sum(jnp.where(eye, col, 0.0), axis=0, keepdims=True)

    def as_col(row):
        return jnp.sum(jnp.where(eye, row, 0.0), axis=1, keepdims=True)

    barrier = pltpu.get_barrier_semaphore()
    partners = (right, left, across, up, down, mate, r1, r2, r3, w_to[1], w_to[3])
    for partner in partners:
        pl.semaphore_signal(
            barrier, inc=1, device_id=partner, device_id_type=pl.DeviceIdType.MESH
        )
    own, own_o = wa.at[zl, y, c], wb.at[zl, y, c]
    places = [(ref, own.at[:, 256 * i : 256 * i + 256]) for i, ref in enumerate((wq, wk, wv))]
    places += [(wo, own_o), (rows_h, rows), (cot_h, cot)]
    places += [(mgain_h, gains.at[0]), (cgain_h, gains.at[1]), (rows_h.at[side], act.at[side, x, zh])]
    fetch = [
        pltpu.make_async_copy(src, dst, lsem.at[i]) for i, (src, dst) in enumerate(places)
    ]
    fetch_cot = pltpu.make_async_copy(cot_h.at[1], act.at[2, x, zh], lsem.at[len(fetch)])
    for one in fetch:
        one.start()
    encoder, decoder = side == 0, side == 1

    @pl.when(decoder)
    def _():
        fetch_cot.start()

    for one in fetch[:4]:
        one.wait()
    pl.semaphore_wait(barrier, len(partners))

    waits = {0: [], 1: []}

    def send_when(of_side, copies):
        @pl.when(side == of_side)
        def _():
            for one in copies:
                one.start()

        waits[of_side].extend(copies)

    def ring_block(t, d):
        return wa.at[zl_of[d], (y + NY + t) % NY, c]

    def forward(t, d):
        if 0 < t < 4 or (t == 4 and d < 2):
            arrived(ring_block(-t, d), Q_UP + 4 * (t - 1) + d)
        if t < 3 or (t == 3 and d < 2):
            send(ring_block(-t, d), ring_block(-t, d), Q_UP + 4 * t + d, up)
        if 0 < t < 4 or (t == 4 and d >= 2):
            arrived(ring_block(t, d), Q_DOWN + 4 * (t - 1) + d)
        if t < 3 or (t == 3 and d >= 2):
            send(ring_block(t, d), ring_block(t, d), Q_DOWN + 4 * t + d, down)

    def from_z(d):
        arrived(ring_block(0, d), Q_Z + d - 1)
        forward(0, d)

    def share(t):
        block = wa.at[:, (y + NY + t) % NY, c]
        send(block, block, Q_MATE + t % NY, mate)

    def out_block(t, half=None):
        parts = slice(0, 4) if half is None else slice(2 * half, 2 * half + 2)
        return wb.at[parts, (y + NY + t) % NY, c]

    def forward_out(t):
        half = (0, 1) if t >= 3 else (None, None)
        took = (0, 1) if t == 4 else (None, None)
        for step, number, to, i in ((-t, O_UP, up, 0), (t, O_DOWN, down, 1)):
            if t > 0:
                arrived(out_block(step, took[i]), number + t - 1)
            if t < 4:
                block = out_block(step, half[i])
                send(block, block, number + t, to)

    def share_out(t):
        block = wb.at[:, (y + NY + t) % NY, c]
        send(block, block, O_MATE + t % NY, mate)

    peers = (right, left, across)
    z_peers = ((r1, other), (r2, side), (r3, other))
    mine, my_cot, my_aux = act.at[side, x, zh], act.at[2, x, zh], aux.at[x, zh]
    kinds = (side, other, side, other)
    z_of = (zh, zh, oh, oh)
    cot_side = (1, 0, 1, 0)
    ring = (xl, xr, xx)

    def rows_block(s, x_):
        return act.at[kinds[s], x_, z_of[s]]

    def cot_block(s, x_):
        return act.at[2, x_, z_of[s]]

    def rows_arrived(s, i):
        arrived(rows_block(s, ring[i]), X_ROWS + 3 * s + i)

    def cot_arrived(s, i):
        @pl.when(side == cot_side[s])
        def _():
            arrived(cot_block(s, ring[i]), X_COT + 3 * s + i)

    def rows_along_x(s):
        block = rows_block(s, x)
        arrived(block, A_ROWS + s - 1)
        for i in range(2):
            send(block, block, X_ROWS + 3 * s + i, peers[i])

    def cot_along_x(s):
        block = cot_block(s, x)

        @pl.when(side == cot_side[s])
        def _():
            arrived(block, A_COT + s - 1)

        send_when(cot_side[s], [copy(block, block, X_COT + 3 * s + i, peers[i]) for i in range(2)])

    def rows_relay(s):
        i = 1 if s == 3 else 0
        rows_arrived(s, i)
        block = rows_block(s, ring[i])
        send(block, block, X_ROWS + 3 * s + 2, peers[i])

    def cot_relay(s):
        i = 0 if s == 3 else 1
        cot_arrived(s, i)
        block = cot_block(s, ring[i])
        send_when(cot_side[s], [copy(block, block, X_COT + 3 * s + 2, peers[i])])

    def make_aux():
        for one in fetch[4:]:
            one.wait()

        @pl.when(decoder)
        def _():
            fetch_cot.wait()

        @pl.when(encoder)
        def _():
            aux[x, zh, 0:1, :] = gains[0]
            aux[x, zh, 1:2, :] = gains[1]
            for m in range(2):
                inner = rows[m].astype(F32) * cot[m].astype(F32) * gains[0]
                aux[x, zh, 2:3, 128 * m : 128 * m + 128] = as_row(
                    jnp.sum(inner, axis=1, keepdims=True)
                )
            aux[x, zh, 3:8, :] = jnp.zeros((5, 256), F32)

        send_when(0, [copy(my_aux, my_aux, A_AUX + i, to) for i, to in enumerate((r1, r2, r3))])

    def aux_along_x():
        @pl.when(encoder)
        def _():
            arrived(aux.at[x, oh], A_AUX + 1)

        @pl.when(decoder)
        def _():
            arrived(aux.at[x, zh], A_AUX)
            arrived(aux.at[x, oh], A_AUX + 2)

        for i, to in enumerate(peers):
            send(aux.at[x], aux.at[x], X_AUX + i, to)

    forward(0, 0)
    for d in (1, 2, 3):
        send(own, own, Q_Z + d - 1, w_to[d])
    for i, to in enumerate(peers):
        send(rows_h.at[side], mine, X_ROWS + i, to)
    send_when(1, [copy(cot_h.at[1], my_cot, X_COT + i, to) for i, to in enumerate(peers)])
    forward(1, 0)
    for d in (1, 2, 3):
        send(own_o, own_o, O_Z + d - 1, w_to[d])
    from_z(1)
    forward(2, 0)
    from_z(2)
    from_z(3)
    for i in (0, 2, 1):
        to, m = z_peers[i]
        send(rows_h.at[m], mine, A_ROWS + i, to)
    make_aux()
    share(0)
    forward(3, 0)
    for d in (1, 2, 3):
        forward(1, d)
    share(1)
    share(-1)
    for d in (1, 2, 3):
        arrived(wb.at[zl_of[d], y, c], O_Z + d - 1)
    forward_out(0)
    send_when(1, [copy(cot_h.at[z_peers[i][1]], my_cot, A_COT + i, z_peers[i][0]) for i in (0, 2, 1)])
    for d in (1, 2, 3):
        forward(2, d)
    share(2)
    share(-2)
    rows_along_x(1)
    rows_along_x(3)
    aux_along_x()
    forward_out(1)
    rows_along_x(2)
    for d in (1, 2, 3):
        forward(3, d)
    share(3)
    share(-3)
    rows_relay(1)
    rows_relay(3)
    forward_out(2)
    for s in (1, 3, 2):
        cot_along_x(s)
    rows_relay(2)
    for d in range(4):
        forward(4, d)
    share(4)
    forward_out(3)
    for s in (1, 3, 2):
        cot_relay(s)
    for t in (0, 1, -1, 2, -2, 3, -3):
        share_out(t)
    forward_out(4)
    share_out(4)

    for i in range(3):
        rows_arrived(0, i)
        arrived(aux.at[ring[i]], X_AUX + i)
    for s, first in ((1, 0), (2, 0), (3, 1)):
        rows_arrived(s, 1 - first)
        rows_arrived(s, 2)
    for t in range(NY):
        arrived(wa.at[:, (y + t) % NY, 1 - c], Q_MATE + t)

    blocks = [(i // 2, i % 2) for i in range(8)]

    def inverse(kind):
        total = jnp.zeros((128, 256), F32)
        for i, j in blocks:
            v = act[kind, i, j].astype(F32)
            total = total + v * v
        return lax.rsqrt(jnp.sum(total, axis=1, keepdims=True) / D + EPS)

    inv_e = inverse(0)
    inv_x = inverse(1)
    kv = jnp.zeros((128, 512), F32)
    q = jnp.zeros((128, 256), F32)
    c_inner = jnp.zeros((1, 256), F32)
    for i, j in blocks:
        memory = (act[0, i, j].astype(F32) * inv_e * aux[i, j, 0:1, :]).astype(BF16)
        normed = (act[1, i, j].astype(F32) * inv_x * aux[i, j, 1:2, :]).astype(BF16)
        part = wa.at[i, 4 * j : 4 * j + 4]
        kv = kv + dot(memory, part[:, :, :, 256:768].reshape(256, 512))
        q = q + dot(normed, part[:, :, :, 0:256].reshape(256, 256))
        c_inner = c_inner + aux[i, j, 2:3, :]
    kv = kv.astype(BF16).astype(F32)
    q = q.astype(BF16).astype(F32)
    c_inner = jnp.where(side == 0, c_inner[:, 0:128], c_inner[:, 128:256])

    low = lax.broadcasted_iota(jnp.int32, (128, 128), 1) < HS
    factor = HS ** (-0.5)

    def two(v):
        return jnp.concatenate(
            [jnp.where(low, v, 0.0).astype(BF16), jnp.where(low, 0.0, v).astype(BF16)], axis=0
        )

    attended, saved = [], []
    for pair in range(2):
        lanes = slice(128 * pair, 128 * pair + 128)
        q2 = two(q[:, lanes])
        key = kv[:, lanes].astype(BF16)
        value = kv[:, 256 + 128 * pair : 384 + 128 * pair]
        scores = dot(q2, key, NT) * factor
        e = jnp.exp(scores - jnp.max(scores, axis=1, keepdims=True))
        probs = e / jnp.sum(e, axis=1, keepdims=True)
        probs_low = probs.astype(BF16)
        v2 = two(value)
        attended.append(dot(probs_low[:128], v2[:128]) + dot(probs_low[128:], v2[128:]))
        saved.append((q2, value.astype(BF16), probs, probs_low))
    attended = jnp.concatenate(attended, axis=1).astype(BF16)

    for t in range(NY):
        arrived(wb.at[:, (y + t) % NY, 1 - c], O_MATE + t)

    def hand_out(kind, chunk):
        base = S_OUT + 6 * kind
        for i, (x_, z_, to, dst) in enumerate(
            (
                (xx, oh, right, far.at[kind, 0]),
                (xx, zh, left, far.at[kind, 1]),
                (xr, zh, right, near.at[kind, 0]),
                (xl, oh, left, near.at[kind, 1]),
            )
        ):
            stage[kind, i] = chunk(x_, z_).astype(BF16)
            send(stage.at[kind, i], dst, base + i, to)
        for i, (x_, z_) in enumerate(((xr, oh), (xl, zh), (x, oh), (x, zh))):
            hold[kind, i] = chunk(x_, z_)

    def pass_on(kind):
        base = S_OUT + 6 * kind
        for i, to in enumerate((right, left)):
            arrived(far.at[kind, i], base + i)
            stage[kind, 4 + i] = (hold[kind, i] + far[kind, i].astype(F32)).astype(BF16)
            send(stage.at[kind, 4 + i], near.at[kind, 2 + i], base + 4 + i, to)

    def finish(kind):
        base = S_OUT + 6 * kind
        for j, pair in enumerate(((1, 2), (0, 3))):
            total = hold[kind, 2 + j]
            for i in pair:
                arrived(near.at[kind, i], base + 2 + i)
                total = total + near[kind, i].astype(F32)
            hold[kind, 2 + j] = total
            last[kind, j] = total.astype(BF16)
            if j == 0:
                slot = 2 - side if kind else 1 + side
                send(
                    last.at[kind, 0], last_in.at[slot], F_SUM + slot,
                    at(zl_=p + 2 * kind, zh_=oh),
                )
            else:
                send_when(1 - kind, [copy(last.at[kind, 1], last_in.at[0], F_SUM, r1)])

    hand_out(1, lambda x_, j: dot(attended, wb[x_, pl.ds(4 * j, 4)].reshape(256, 256), NT))

    for i in range(3):
        cot_arrived(0, i)
    for s, first in ((1, 1), (2, 1), (3, 0)):
        cot_arrived(s, 1 - first)
        cot_arrived(s, 2)
    da = jnp.zeros((128, 256), F32)
    for i, j in blocks:
        da = da + dot(act[2, i, j], wb[i, 4 * j : 4 * j + 4].reshape(256, 256))
    da = da.astype(BF16).astype(F32)

    d_keys, d_values = [], []
    for pair, (q2, value, probs, probs_low) in enumerate(saved):
        da2 = two(da[:, 128 * pair : 128 * pair + 128])
        d_probs = dot(da2, value, NT)
        d_scores = probs * (d_probs - jnp.sum(probs * d_probs, axis=1, keepdims=True))
        d_low = (d_scores * factor).astype(BF16)
        d_keys.append(dot(d_low, q2, TN))
        d_values.append(dot(probs_low, da2, TN))
    d_kv = jnp.concatenate(d_keys + d_values, axis=1).astype(BF16)
    pass_on(1)
    inner = [jnp.zeros((128, 256), F32)]

    def memory_chunk(x_, j):
        v = dot(d_kv, wa[x_, pl.ds(4 * j, 4), :, :, 256:768].reshape(256, 512), NT)
        inner[0] = inner[0] + v * (act[0, x_, j].astype(F32) * aux[x_, j, 0:1, :])
        return v

    hand_out(0, memory_chunk)
    own_inner = as_row(jnp.sum(inner[0], axis=1, keepdims=True))
    stat_out[0:1, :] = own_inner
    stat_out[1:8, :] = jnp.zeros((7, 128), F32)
    for i, to in enumerate((right, left, across)):
        send(stat_out, stat_in.at[i], S_STAT + i, to)
    pass_on(0)

    finish(1)
    for i in range(3):
        arrived(stat_in.at[i], S_STAT + i)
    part_inner = own_inner
    for i in range(3):
        part_inner = part_inner + stat_in[i, 0:1, :]
    part_inner = part_inner + jnp.where(zh == 0, c_inner, 0.0)
    last_stat[0:1, :] = part_inner
    last_stat[1:2, :] = as_row(inv_e)
    last_stat[2:8, :] = jnp.zeros((6, 128), F32)
    for i, to in enumerate((r1, r2, r3)):
        send(last_stat, stat_last.at[i], F_STAT + i, to)
    finish(0)

    for i in range(3):
        arrived(stat_last.at[i], F_STAT + i)
        arrived(last_in.at[i], F_SUM + i)
    sums = (
        hold[side, 3] + last_in[1].astype(F32),
        last_in[0].astype(F32) + last_in[2].astype(F32),
    )

    @pl.when(side == 1)
    def _():
        for m, total in ((1, sums[0]), (0, sums[1])):
            out[m] = (rows[m].astype(F32) + total).astype(BF16)

    @pl.when(side == 0)
    def _():
        inners = (
            part_inner + stat_last[1, 0:1, :],
            stat_last[0, 0:1, :] + stat_last[2, 0:1, :],
        )
        invs = (inv_e, as_col(stat_last[0, 1:2, :]))
        for m in range(2):
            weighted = (sums[m] + cot[m].astype(F32)) * gains[0]
            mean = as_col(inners[m]) / D
            inv = invs[m]
            d_rows = inv * weighted - rows[m].astype(F32) * (inv * inv * inv * mean)
            out[m] = d_rows.astype(BF16)

    for one in pending:
        one.wait_send()
    for of_side in (0, 1):

        @pl.when(side == of_side)
        def _(of_side=of_side):
            for one in waits[of_side]:
                one.wait_send()


def local(segment_rows, row_cotangent, memory_gain, cross_gain, w_query, w_key, w_value, w_out):
    return pl.pallas_call(
        kernel,
        out_shape=jax.ShapeDtypeStruct((2, 128, 256), BF16),
        in_specs=[pl.BlockSpec(memory_space=pl.ANY)] * 8,
        out_specs=pl.BlockSpec(memory_space=pltpu.VMEM),
        scratch_shapes=[
            pltpu.VMEM((2, 128, 256), BF16),
            pltpu.VMEM((2, 128, 256), BF16),
            pltpu.VMEM((2, 1, 256), F32),
            pltpu.VMEM((4, NY, 2, 32, 768), BF16),
            pltpu.VMEM((4, NY, 2, 32, 256), BF16),
            pltpu.VMEM((3, NX, 2, 128, 256), BF16),
            pltpu.VMEM((NX, 2, 8, 256), F32),
            pltpu.VMEM((2, 4, 128, 256), F32),
            pltpu.VMEM((2, 6, 128, 256), BF16),
            pltpu.VMEM((2, 4, 128, 256), BF16),
            pltpu.VMEM((2, 2, 128, 256), BF16),
            pltpu.VMEM((8, 128), F32),
            pltpu.VMEM((3, 8, 128), F32),
            pltpu.VMEM((2, 2, 128, 256), BF16),
            pltpu.VMEM((3, 128, 256), BF16),
            pltpu.VMEM((8, 128), F32),
            pltpu.VMEM((3, 8, 128), F32),
            pltpu.SemaphoreType.DMA((10,)),
            pltpu.SemaphoreType.DMA((COPIES,)),
            pltpu.SemaphoreType.DMA((COPIES,)),
        ],
        compiler_params=pltpu.CompilerParams(
            collective_id=0, has_side_effects=True, vmem_limit_bytes=60 * 1024 * 1024
        ),
    )(
        segment_rows, row_cotangent, memory_gain.reshape(1, -1), cross_gain.reshape(1, -1),
        w_query, w_key, w_value, w_out.T,
    )


def solution(mesh):
    in_specs = (
        P(None, "segment", "head"),
        P(None, "segment", "head"),
        P("head"),
        P("head"),
        P("segment", "head"),
        P("segment", "head"),
        P("segment", "head"),
        P("head", "segment"),
    )
    out_specs = P(None, "segment", "head")
    return jax.shard_map(local, mesh=mesh, in_specs=in_specs, out_specs=out_specs, check_vma=False)
```

time: 77.7 us -> 67.6 us (0.87)
  the two profiles are of different devices: /device:TPU:19 before, /device:TPU:8 now
where the time goes in v2:
time: 67.6 us; the launch traced here: 67.4 us
  Pallas kernels  65.8 us (97%)
  local copies, waits for them, and re-layouts  1.57 us (2%)
    pallas_call x1, Pallas kernels, local(): pl.pallas_call(kernel, out_shape=jax.ShapeDtypeStruct((2, 128, 256), BF16...  65.8 us
    unnamed x1, local copies, waits for them, and re-layouts  1.57 us

profile of v2, /device:TPU:8, one launch (start us, length us, event | category | flops | bytes accessed | tf_op | source)
XLA Modules:
  0.0 67.4 jit_solution(5432071893108823626)
XLA Ops:
  0.0 65.8 %shard_map.82 = bf16[2,128,256]{2,1,0:T(8,128)(2,1)} custom-call(bf16[2,128,256]{2,1,0:T(8,128)(2,1)} %rows_h.1, bf16[2,128,256]{2,1,0:T(8,128)(2,1)} %cot_h.1, f32[1,256]{1,0:T(1,128)} %bitcast.4, f32[1,256]{1,0:T(1,128)} %bitcast.5, bf16[32,256]{1,0:T(8,128)(2,1)} %wq.1, bf16[32,256]{1,0:T(8,128)(2,1)} %wk.1, bf16[32,256]{1,0:T(8,128)(2,1)} %wv.1, ...), custom_call_target="tpu_custom_call" | custom-call | tf_op jit(solution)/shard_map/pallas_call | solution.py:503
  65.8 1.6 %copy.10 = bf16[2,128,256]{2,1,0:T(8,128)(2,1)} copy(bf16[2,128,256]{2,1,0:T(8,128)(2,1)} %shard_map.82) | data formatting | bytes 262144

commit v3 on v2

--- a/solution.py
+++ b/solution.py
@@ -17,25 +17,22 @@
 F32 = jnp.float32
 BF16 = jnp.bfloat16
 
-Q_Z = 0
-Q_UP = 3
-Q_DOWN = 19
-Q_MATE = 35
-O_Z = 43
-O_UP = 46
-O_DOWN = 50
-O_MATE = 54
-A_ROWS = 62
-A_COT = 65
-A_AUX = 68
-X_ROWS = 71
-X_COT = 83
-X_AUX = 95
-S_OUT = 98
-S_STAT = 110
-F_SUM = 113
-F_STAT = 116
-COPIES = 119
+W_Z = 0
+W_UP = 3
+W_DOWN = 19
+W_MATE = 35
+W_LAST = 43
+A_ROWS = 47
+A_COT = 50
+A_AUX = 53
+X_ROWS = 56
+X_COT = 68
+X_AUX = 80
+S_OUT = 83
+S_STAT = 95
+F_SUM = 98
+F_STAT = 101
+COPIES = 104
 
 
 def dot(a, b, dims=(((1,), (0,)), ((), ()))):
@@ -44,7 +41,7 @@
 
 def kernel(
     rows_h, cot_h, mgain_h, cgain_h, wq, wk, wv, wo, out,
-    rows, cot, gains, wa, wb, act, aux, hold, stage, near, far, stat_out, stat_in, last, last_in, last_stat,
+    rows, cot, gains, w, act, aux, hold, stage, near, far, stat_out, stat_in, last, last_in, last_stat,
     stat_last, lsem, ssem, rsem,
 ):
     seg = lax.axis_index("segment")
@@ -102,9 +99,9 @@
         pl.semaphore_signal(
             barrier, inc=1, device_id=partner, device_id_type=pl.DeviceIdType.MESH
         )
-    own, own_o = wa.at[zl, y, c], wb.at[zl, y, c]
-    places = [(ref, own.at[:, 256 * i : 256 * i + 256]) for i, ref in enumerate((wq, wk, wv))]
-    places += [(wo, own_o), (rows_h, rows), (cot_h, cot)]
+    own = w.at[zl, y, c]
+    places = [(ref, own.at[:, 256 * i : 256 * i + 256]) for i, ref in enumerate((wq, wk, wv, wo))]
+    places += [(rows_h, rows), (cot_h, cot)]
     places += [(mgain_h, gains.at[0]), (cgain_h, gains.at[1]), (rows_h.at[side], act.at[side, x, zh])]
     fetch = [
         pltpu.make_async_copy(src, dst, lsem.at[i]) for i, (src, dst) in enumerate(places)
@@ -133,43 +130,29 @@
         waits[of_side].extend(copies)
 
     def ring_block(t, d):
-        return wa.at[zl_of[d], (y + NY + t) % NY, c]
+        return w.at[zl_of[d], (y + NY + t) % NY, c]
 
     def forward(t, d):
         if 0 < t < 4 or (t == 4 and d < 2):
-            arrived(ring_block(-t, d), Q_UP + 4 * (t - 1) + d)
+            arrived(ring_block(-t, d), W_UP + 4 * (t - 1) + d)
         if t < 3 or (t == 3 and d < 2):
-            send(ring_block(-t, d), ring_block(-t, d), Q_UP + 4 * t + d, up)
+            send(ring_block(-t, d), ring_block(-t, d), W_UP + 4 * t + d, up)
         if 0 < t < 4 or (t == 4 and d >= 2):
-            arrived(ring_block(t, d), Q_DOWN + 4 * (t - 1) + d)
+            arrived(ring_block(t, d), W_DOWN + 4 * (t - 1) + d)
         if t < 3 or (t == 3 and d >= 2):
-            send(ring_block(t, d), ring_block(t, d), Q_DOWN + 4 * t + d, down)
+            send(ring_block(t, d), ring_block(t, d), W_DOWN + 4 * t + d, down)
 
     def from_z(d):
-        arrived(ring_block(0, d), Q_Z + d - 1)
+        arrived(ring_block(0, d), W_Z + d - 1)
         forward(0, d)
 
     def share(t):
-        block = wa.at[:, (y + NY + t) % NY, c]
-        send(block, block, Q_MATE + t % NY, mate)
-
-    def out_block(t, half=None):
-        parts = slice(0, 4) if half is None else slice(2 * half, 2 * half + 2)
-        return wb.at[parts, (y + NY + t) % NY, c]
-
-    def forward_out(t):
-        half = (0, 1) if t >= 3 else (None, None)
-        took = (0, 1) if t == 4 else (None, None)
-        for step, number, to, i in ((-t, O_UP, up, 0), (t, O_DOWN, down, 1)):
-            if t > 0:
-                arrived(out_block(step, took[i]), number + t - 1)
-            if t < 4:
-                block = out_block(step, half[i])
-                send(block, block, number + t, to)
-
-    def share_out(t):
-        block = wb.at[:, (y + NY + t) % NY, c]
-        send(block, block, O_MATE + t % NY, mate)
+        block = w.at[:, (y + NY + t) % NY, c]
+        send(block, block, W_MATE + t % NY, mate)
+
+    def share_block(t, d):
+        block = ring_block(t, d)
+        send(block, block, W_LAST + d, mate)
 
     peers = (right, left, across)
     z_peers = ((r1, other), (r2, side), (r3, other))
@@ -256,60 +239,51 @@
 
     forward(0, 0)
     for d in (1, 2, 3):
-        send(own, own, Q_Z + d - 1, w_to[d])
+        send(own, own, W_Z + d - 1, w_to[d])
     for i, to in enumerate(peers):
         send(rows_h.at[side], mine, X_ROWS + i, to)
     send_when(1, [copy(cot_h.at[1], my_cot, X_COT + i, to) for i, to in enumerate(peers)])
-    forward(1, 0)
-    for d in (1, 2, 3):
-        send(own_o, own_o, O_Z + d - 1, w_to[d])
     from_z(1)
-    forward(2, 0)
     from_z(2)
     from_z(3)
     for i in (0, 2, 1):
         to, m = z_peers[i]
         send(rows_h.at[m], mine, A_ROWS + i, to)
     make_aux()
+    send_when(1, [copy(cot_h.at[z_peers[i][1]], my_cot, A_COT + i, z_peers[i][0]) for i in (0, 2, 1)])
     share(0)
-    forward(3, 0)
-    for d in (1, 2, 3):
-        forward(1, d)
+    forward(1, 0)
+    forward(1, 1)
+    forward(1, 2)
+    forward(1, 3)
     share(1)
     share(-1)
-    for d in (1, 2, 3):
-        arrived(wb.at[zl_of[d], y, c], O_Z + d - 1)
-    forward_out(0)
-    send_when(1, [copy(cot_h.at[z_peers[i][1]], my_cot, A_COT + i, z_peers[i][0]) for i in (0, 2, 1)])
-    for d in (1, 2, 3):
-        forward(2, d)
+    forward(2, 0)
+    forward(2, 1)
+    forward(2, 2)
+    forward(2, 3)
     share(2)
     share(-2)
     rows_along_x(1)
     rows_along_x(3)
     aux_along_x()
-    forward_out(1)
     rows_along_x(2)
-    for d in (1, 2, 3):
-        forward(3, d)
+    forward(3, 0)
+    forward(3, 1)
+    forward(3, 2)
+    forward(3, 3)
     share(3)
     share(-3)
     rows_relay(1)
     rows_relay(3)
-    forward_out(2)
     for s in (1, 3, 2):
         cot_along_x(s)
     rows_relay(2)
     for d in range(4):
         forward(4, d)
-    share(4)
-    forward_out(3)
+        share_block(4, d)
     for s in (1, 3, 2):
         cot_relay(s)
-    for t in (0, 1, -1, 2, -2, 3, -3):
-        share_out(t)
-    forward_out(4)
-    share_out(4)
 
     for i in range(3):
         rows_arrived(0, i)
@@ -318,7 +292,11 @@
         rows_arrived(s, 1 - first)
         rows_arrived(s, 2)
     for t in range(NY):
-        arrived(wa.at[:, (y + t) % NY, 1 - c], Q_MATE + t)
+        if t == 4:
+            for d in range(4):
+                arrived(w.at[zl_of[d], (y + 4) % NY, 1 - c], W_LAST + d)
+        else:
+            arrived(w.at[:, (y + t) % NY, 1 - c], W_MATE + t)
 
     blocks = [(i // 2, i % 2) for i in range(8)]
 
@@ -337,7 +315,7 @@
     for i, j in blocks:
         memory = (act[0, i, j].astype(F32) * inv_e * aux[i, j, 0:1, :]).astype(BF16)
         normed = (act[1, i, j].astype(F32) * inv_x * aux[i, j, 1:2, :]).astype(BF16)
-        part = wa.at[i, 4 * j : 4 * j + 4]
+        part = w.at[i, 4 * j : 4 * j + 4]
         kv = kv + dot(memory, part[:, :, :, 256:768].reshape(256, 512))
         q = q + dot(normed, part[:, :, :, 0:256].reshape(256, 256))
         c_inner = c_inner + aux[i, j, 2:3, :]
@@ -367,9 +345,6 @@
         attended.append(dot(probs_low[:128], v2[:128]) + dot(probs_low[128:], v2[128:]))
         saved.append((q2, value.astype(BF16), probs, probs_low))
     attended = jnp.concatenate(attended, axis=1).astype(BF16)
-
-    for t in range(NY):
-        arrived(wb.at[:, (y + t) % NY, 1 - c], O_MATE + t)
 
     def hand_out(kind, chunk):
         base = S_OUT + 6 * kind
@@ -411,7 +386,7 @@
             else:
                 send_when(1 - kind, [copy(last.at[kind, 1], last_in.at[0], F_SUM, r1)])
 
-    hand_out(1, lambda x_, j: dot(attended, wb[x_, pl.ds(4 * j, 4)].reshape(256, 256), NT))
+    hand_out(1, lambda x_, j: dot(attended, w[x_, pl.ds(4 * j, 4), :, :, 768:1024].reshape(256, 256), NT))
 
     for i in range(3):
         cot_arrived(0, i)
@@ -420,7 +395,7 @@
         cot_arrived(s, 2)
     da = jnp.zeros((128, 256), F32)
     for i, j in blocks:
-        da = da + dot(act[2, i, j], wb[i, 4 * j : 4 * j + 4].reshape(256, 256))
+        da = da + dot(act[2, i, j], w[i, 4 * j : 4 * j + 4, :, :, 768:1024].reshape(256, 256))
     da = da.astype(BF16).astype(F32)
 
     d_keys, d_values = [], []
@@ -436,7 +411,7 @@
     inner = [jnp.zeros((128, 256), F32)]
 
     def memory_chunk(x_, j):
-        v = dot(d_kv, wa[x_, pl.ds(4 * j, 4), :, :, 256:768].reshape(256, 512), NT)
+        v = dot(d_kv, w[x_, pl.ds(4 * j, 4), :, :, 256:768].reshape(256, 512), NT)
         inner[0] = inner[0] + v * (act[0, x_, j].astype(F32) * aux[x_, j, 0:1, :])
         return v
 
@@ -499,6 +474,10 @@
                 one.wait_send()
 
 
+def hb(v):
+    return pltpu.with_memory_space_constraint(v, pltpu.HBM)
+
+
 def local(segment_rows, row_cotangent, memory_gain, cross_gain, w_query, w_key, w_value, w_out):
     return pl.pallas_call(
         kernel,
@@ -509,8 +488,7 @@
             pltpu.VMEM((2, 128, 256), BF16),
             pltpu.VMEM((2, 128, 256), BF16),
             pltpu.VMEM((2, 1, 256), F32),
-            pltpu.VMEM((4, NY, 2, 32, 768), BF16),
-            pltpu.VMEM((4, NY, 2, 32, 256), BF16),
+            pltpu.VMEM((4, NY, 2, 32, 1024), BF16),
             pltpu.VMEM((3, NX, 2, 128, 256), BF16),
             pltpu.VMEM((NX, 2, 8, 256), F32),
             pltpu.VMEM((2, 4, 128, 256), F32),
@@ -528,11 +506,11 @@
             pltpu.SemaphoreType.DMA((COPIES,)),
         ],
         compiler_params=pltpu.CompilerParams(
-            collective_id=0, has_side_effects=True, vmem_limit_bytes=60 * 1024 * 1024
+            collective_id=0, has_side_effects=True, vmem_limit_bytes=48 * 1024 * 1024
         ),
     )(
-        segment_rows, row_cotangent, memory_gain.reshape(1, -1), cross_gain.reshape(1, -1),
-        w_query, w_key, w_value, w_out.T,
+        hb(segment_rows), hb(row_cotangent), hb(memory_gain.reshape(1, -1)), hb(cross_gain.reshape(1, -1)),
+        hb(w_query), hb(w_key), hb(w_value), hb(w_out.T),
     )
 
 

time: 67.6 us -> 63.8 us (0.944)
  the two profiles are of different devices: /device:TPU:8 before, /device:TPU:2 now
where the time goes in v3:
time: 63.8 us; the launch traced here: 63.6 us
  Pallas kernels  62.9 us (99%)
  local copies, waits for them, and re-layouts  0.66 us (1%)
    pallas_call x1, Pallas kernels, local(): pl.pallas_call(kernel, out_shape=jax.ShapeDtypeStruct((2, 128, 256), BF16...  62.9 us

profile of v3, /device:TPU:2, one launch (start us, length us, event | category | flops | bytes accessed | tf_op | source)
XLA Modules:
  0.0 63.6 jit_solution(11922937759124994799)
XLA Ops:
  0.0 62.9 %shard_map.82 = bf16[2,128,256]{2,1,0:T(8,128)(2,1)S(1)} custom-call(bf16[2,128,256]{2,1,0:T(8,128)(2,1)} %rows_h.1, bf16[2,128,256]{2,1,0:T(8,128)(2,1)} %cot_h.1, f32[1,256]{1,0:T(1,128)} %bitcast.4, f32[1,256]{1,0:T(1,128)} %bitcast.5, bf16[32,256]{1,0:T(8,128)(2,1)} %wq.1, bf16[32,256]{1,0:T(8,128)(2,1)} %wk.1, bf16[32,256]{1,0:T(8,128)(2,1)} %wv.1, ...), custom_call_target="tpu_custom_call" | custom-call | tf_op jit(solution)/shard_map/pallas_call | solution.py:482
  62.9 0.7 %copy.10 = bf16[2,128,256]{2,1,0:T(8,128)(2,1)} copy(bf16[2,128,256]{2,1,0:T(8,128)(2,1)S(1)} %shard_map.82) | data formatting | bytes 262144

commit v4 on v3

--- a/solution.py
+++ b/solution.py
@@ -33,6 +33,10 @@
 F_SUM = 98
 F_STAT = 101
 COPIES = 104
+
+
+DIRECT_ROWS = ()
+DIRECT_COT = ()
 
 
 def dot(a, b, dims=(((1,), (0,)), ((), ()))):
@@ -176,10 +180,18 @@
         def _():
             arrived(cot_block(s, ring[i]), X_COT + 3 * s + i)
 
+    def rows_along_z(i):
+        to, m = z_peers[i]
+        send(rows_h.at[m], mine, A_ROWS + i, to)
+
+    def cot_along_z(i):
+        to, m = z_peers[i]
+        send_when(1, [copy(cot_h.at[m], my_cot, A_COT + i, to)])
+
     def rows_along_x(s):
         block = rows_block(s, x)
         arrived(block, A_ROWS + s - 1)
-        for i in range(2):
+        for i in (0, 1) if s not in DIRECT_ROWS else (2, 0, 1):
             send(block, block, X_ROWS + 3 * s + i, peers[i])
 
     def cot_along_x(s):
@@ -189,7 +201,7 @@
         def _():
             arrived(block, A_COT + s - 1)
 
-        send_when(cot_side[s], [copy(block, block, X_COT + 3 * s + i, peers[i]) for i in range(2)])
+        send_when(cot_side[s], [copy(block, block, X_COT + 3 * s + i, peers[i]) for i in ((0, 1) if s not in DIRECT_COT else (2, 0, 1))])
 
     def rows_relay(s):
         i = 1 if s == 3 else 0
@@ -246,11 +258,13 @@
     from_z(1)
     from_z(2)
     from_z(3)
-    for i in (0, 2, 1):
-        to, m = z_peers[i]
-        send(rows_h.at[m], mine, A_ROWS + i, to)
+    rows_along_z(0)
+    rows_along_z(2)
+    rows_along_z(1)
+    cot_along_z(1)
     make_aux()
-    send_when(1, [copy(cot_h.at[z_peers[i][1]], my_cot, A_COT + i, z_peers[i][0]) for i in (0, 2, 1)])
+    cot_along_z(0)
+    cot_along_z(2)
     share(0)
     forward(1, 0)
     forward(1, 1)
@@ -276,21 +290,46 @@
     share(-3)
     rows_relay(1)
     rows_relay(3)
-    for s in (1, 3, 2):
-        cot_along_x(s)
+    cot_along_x(1)
+    cot_along_x(3)
+    cot_along_x(2)
     rows_relay(2)
-    for d in range(4):
-        forward(4, d)
-        share_block(4, d)
-    for s in (1, 3, 2):
-        cot_relay(s)
+    forward(4, 0)
+    share_block(4, 0)
+    forward(4, 1)
+    share_block(4, 1)
+    forward(4, 2)
+    share_block(4, 2)
+    forward(4, 3)
+    share_block(4, 3)
+    cot_relay(1)
+    cot_relay(3)
+    cot_relay(2)
 
     for i in range(3):
         rows_arrived(0, i)
         arrived(aux.at[ring[i]], X_AUX + i)
     for s, first in ((1, 0), (2, 0), (3, 1)):
-        rows_arrived(s, 1 - first)
-        rows_arrived(s, 2)
+        for i in range(3):
+            if s in DIRECT_ROWS or i != first:
+                rows_arrived(s, i)
+    blocks = [(i // 2, i % 2) for i in range(8)]
+
+    def inverse(kind):
+        total = jnp.zeros((128, 256), F32)
+        for i, j in blocks:
+            v = act[kind, i, j].astype(F32)
+            total = total + v * v
+        return lax.rsqrt(jnp.sum(total, axis=1, keepdims=True) / D + EPS)
+
+    inv_e = inverse(0)
+    inv_x = inverse(1)
+    memories = [
+        (act[0, i, j].astype(F32) * inv_e * aux[i, j, 0:1, :]).astype(BF16) for i, j in blocks
+    ]
+    normeds = [
+        (act[1, i, j].astype(F32) * inv_x * aux[i, j, 1:2, :]).astype(BF16) for i, j in blocks
+    ]
     for t in range(NY):
         if t == 4:
             for d in range(4):
@@ -298,23 +337,10 @@
         else:
             arrived(w.at[:, (y + t) % NY, 1 - c], W_MATE + t)
 
-    blocks = [(i // 2, i % 2) for i in range(8)]
-
-    def inverse(kind):
-        total = jnp.zeros((128, 256), F32)
-        for i, j in blocks:
-            v = act[kind, i, j].astype(F32)
-            total = total + v * v
-        return lax.rsqrt(jnp.sum(total, axis=1, keepdims=True) / D + EPS)
-
-    inv_e = inverse(0)
-    inv_x = inverse(1)
     kv = jnp.zeros((128, 512), F32)
     q = jnp.zeros((128, 256), F32)
     c_inner = jnp.zeros((1, 256), F32)
-    for i, j in blocks:
-        memory = (act[0, i, j].astype(F32) * inv_e * aux[i, j, 0:1, :]).astype(BF16)
-        normed = (act[1, i, j].astype(F32) * inv_x * aux[i, j, 1:2, :]).astype(BF16)
+    for (i, j), memory, normed in zip(blocks, memories, normeds):
         part = w.at[i, 4 * j : 4 * j + 4]
         kv = kv + dot(memory, part[:, :, :, 256:768].reshape(256, 512))
         q = q + dot(normed, part[:, :, :, 0:256].reshape(256, 256))
@@ -358,6 +384,8 @@
         ):
             stage[kind, i] = chunk(x_, z_).astype(BF16)
             send(stage.at[kind, i], dst, base + i, to)
+
+    def keep(kind, chunk):
         for i, (x_, z_) in enumerate(((xr, oh), (xl, zh), (x, oh), (x, zh))):
             hold[kind, i] = chunk(x_, z_)
 
@@ -386,13 +414,17 @@
             else:
                 send_when(1 - kind, [copy(last.at[kind, 1], last_in.at[0], F_SUM, r1)])
 
-    hand_out(1, lambda x_, j: dot(attended, w[x_, pl.ds(4 * j, 4), :, :, 768:1024].reshape(256, 256), NT))
+    def out_chunk(x_, j):
+        return dot(attended, w[x_, pl.ds(4 * j, 4), :, :, 768:1024].reshape(256, 256), NT)
+
+    hand_out(1, out_chunk)
 
     for i in range(3):
         cot_arrived(0, i)
     for s, first in ((1, 1), (2, 1), (3, 0)):
-        cot_arrived(s, 1 - first)
-        cot_arrived(s, 2)
+        for i in range(3):
+            if s in DIRECT_COT or i != first:
+                cot_arrived(s, i)
     da = jnp.zeros((128, 256), F32)
     for i, j in blocks:
         da = da + dot(act[2, i, j], w[i, 4 * j : 4 * j + 4, :, :, 768:1024].reshape(256, 256))
@@ -407,7 +439,6 @@
         d_keys.append(dot(d_low, q2, TN))
         d_values.append(dot(probs_low, da2, TN))
     d_kv = jnp.concatenate(d_keys + d_values, axis=1).astype(BF16)
-    pass_on(1)
     inner = [jnp.zeros((128, 256), F32)]
 
     def memory_chunk(x_, j):
@@ -416,6 +447,9 @@
         return v
 
     hand_out(0, memory_chunk)
+    keep(1, out_chunk)
+    pass_on(1)
+    keep(0, memory_chunk)
     own_inner = as_row(jnp.sum(inner[0], axis=1, keepdims=True))
     stat_out[0:1, :] = own_inner
     stat_out[1:8, :] = jnp.zeros((7, 128), F32)

time: 63.8 us -> 63 us (0.987)
  the two profiles are of different devices: /device:TPU:2 before, /device:TPU:24 now
where the time goes in v4:
time: 63 us; the launch traced here: 62.8 us
  Pallas kernels  62.1 us (99%)
  local copies, waits for them, and re-layouts  0.66 us (1%)
    pallas_call x1, Pallas kernels, local(): pl.pallas_call(kernel, out_shape=jax.ShapeDtypeStruct((2, 128, 256), BF16...  62.1 us

profile of v4, /device:TPU:24, one launch (start us, length us, event | category | flops | bytes accessed | tf_op | source)
XLA Modules:
  0.0 62.8 jit_solution(1715170628069542108)
XLA Ops:
  0.0 62.1 %shard_map.82 = bf16[2,128,256]{2,1,0:T(8,128)(2,1)S(1)} custom-call(bf16[2,128,256]{2,1,0:T(8,128)(2,1)} %rows_h.1, bf16[2,128,256]{2,1,0:T(8,128)(2,1)} %cot_h.1, f32[1,256]{1,0:T(1,128)} %bitcast.4, f32[1,256]{1,0:T(1,128)} %bitcast.5, bf16[32,256]{1,0:T(8,128)(2,1)} %wq.1, bf16[32,256]{1,0:T(8,128)(2,1)} %wk.1, bf16[32,256]{1,0:T(8,128)(2,1)} %wv.1, ...), custom_call_target="tpu_custom_call" | custom-call | tf_op jit(solution)/shard_map/pallas_call | solution.py:516
  62.1 0.7 %copy.10 = bf16[2,128,256]{2,1,0:T(8,128)(2,1)} copy(bf16[2,128,256]{2,1,0:T(8,128)(2,1)S(1)} %shard_map.82) | data formatting | bytes 262144

commit v5 on v4

--- a/solution.py
+++ b/solution.py
@@ -46,7 +46,7 @@
 def kernel(
     rows_h, cot_h, mgain_h, cgain_h, wq, wk, wv, wo, out,
     rows, cot, gains, w, act, aux, hold, stage, near, far, stat_out, stat_in, last, last_in, last_stat,
-    stat_last, lsem, ssem, rsem,
+    stat_last, lsem, ssem, rsem, answer,
 ):
     seg = lax.axis_index("segment")
     head = lax.axis_index("head")
@@ -98,11 +98,20 @@
         return jnp.sum(jnp.where(eye, row, 0.0), axis=1, keepdims=True)
 
     barrier = pltpu.get_barrier_semaphore()
-    partners = (right, left, across, up, down, mate, r1, r2, r3, w_to[1], w_to[3])
-    for partner in partners:
-        pl.semaphore_signal(
-            barrier, inc=1, device_id=partner, device_id_type=pl.DeviceIdType.MESH
-        )
+    partners = (right, left, across, up, down, mate, r1, w_to[1], w_to[3])
+
+    def greet(semaphore, devices):
+        for device in devices:
+            pl.semaphore_signal(
+                semaphore, inc=1, device_id=device, device_id_type=pl.DeviceIdType.MESH
+            )
+
+    greet(barrier, partners)
+
+    @pl.when(zh == 0)
+    def _():
+        greet(barrier, (r2, r3))
+
     own = w.at[zl, y, c]
     places = [(ref, own.at[:, 256 * i : 256 * i + 256]) for i, ref in enumerate((wq, wk, wv, wo))]
     places += [(rows_h, rows), (cot_h, cot)]
@@ -121,7 +130,12 @@
 
     for one in fetch[:4]:
         one.wait()
-    pl.semaphore_wait(barrier, len(partners))
+    pl.semaphore_wait(barrier, len(partners) + 2 * zh)
+
+    @pl.when(zh == 1)
+    def _():
+        greet(answer, (r2, r3))
+
 
     waits = {0: [], 1: []}
 
@@ -258,6 +272,11 @@
     from_z(1)
     from_z(2)
     from_z(3)
+
+    @pl.when(zh == 0)
+    def _():
+        pl.semaphore_wait(answer, 2)
+
     rows_along_z(0)
     rows_along_z(2)
     rows_along_z(1)
@@ -274,12 +293,12 @@
     share(-1)
     forward(2, 0)
     forward(2, 1)
+    rows_along_x(1)
     forward(2, 2)
+    rows_along_x(3)
     forward(2, 3)
     share(2)
     share(-2)
-    rows_along_x(1)
-    rows_along_x(3)
     aux_along_x()
     rows_along_x(2)
     forward(3, 0)
@@ -538,6 +557,7 @@
             pltpu.SemaphoreType.DMA((10,)),
             pltpu.SemaphoreType.DMA((COPIES,)),
             pltpu.SemaphoreType.DMA((COPIES,)),
+            pltpu.SemaphoreType.REGULAR,
         ],
         compiler_params=pltpu.CompilerParams(
             collective_id=0, has_side_effects=True, vmem_limit_bytes=48 * 1024 * 1024

time: 63 us -> 62.4 us (level)
  the two profiles are of different devices: /device:TPU:24 before, /device:TPU:16 now
where the time goes in v5:
time: 62.4 us; the launch traced here: 62.2 us
  Pallas kernels  61.5 us (99%)
  local copies, waits for them, and re-layouts  0.66 us (1%)
    pallas_call x1, Pallas kernels, local(): pl.pallas_call(kernel, out_shape=jax.ShapeDtypeStruct((2, 128, 256), BF16...  61.5 us

profile of v5, /device:TPU:16, one launch (start us, length us, event | category | flops | bytes accessed | tf_op | source)
XLA Modules:
  0.0 62.2 jit_solution(10532935833158709798)
XLA Ops:
  0.0 61.5 %shard_map.82 = bf16[2,128,256]{2,1,0:T(8,128)(2,1)S(1)} custom-call(bf16[2,128,256]{2,1,0:T(8,128)(2,1)} %rows_h.1, bf16[2,128,256]{2,1,0:T(8,128)(2,1)} %cot_h.1, f32[1,256]{1,0:T(1,128)} %bitcast.4, f32[1,256]{1,0:T(1,128)} %bitcast.5, bf16[32,256]{1,0:T(8,128)(2,1)} %wq.1, bf16[32,256]{1,0:T(8,128)(2,1)} %wk.1, bf16[32,256]{1,0:T(8,128)(2,1)} %wv.1, ...), custom_call_target="tpu_custom_call" | custom-call | tf_op jit(solution)/shard_map/pallas_call | solution.py:535
  61.5 0.7 %copy.10 = bf16[2,128,256]{2,1,0:T(8,128)(2,1)} copy(bf16[2,128,256]{2,1,0:T(8,128)(2,1)S(1)} %shard_map.82) | data formatting | bytes 262144
